TPU v7x, 32 devices: a whole 2x2x4 slice. The times are simulated.
32 devices in a mesh: grp: 2 (over x), seq: 16 (over z, y, core).
Axes of the slice: x: 2, y: 2, z: 4, core: 2. Of those that a mesh axis runs over, the one named last changes fastest.
Arguments:
- tokens: bfloat16 [2, 131072, 768], P('grp', 'seq'), parts along dimension 0, may hold values from -36 to 36
- right_factor: bfloat16 [256, 512, 512], P('seq'), may hold values from -0.25 to 0.25
- left_factor: bfloat16 [512, 256, 256], P('seq'), may hold values from -0.375 to 0.375
- twiddle: float32 [256, 512], P('seq'), may hold values from 0.5 to 2
- norm_gain: float32 [768], replicated, may hold values from 0.1 to 1.9
- mix_gain: float32 [768], replicated, may hold values from 0.1 to 1.9
- value_weight: bfloat16 [768, 768], replicated, may hold values from -0.21875 to 0.21875
- gate_weight: bfloat16 [768, 768], replicated, may hold values from -0.21875 to 0.21875
Outputs:
- layer_out: bfloat16 [2, 131072, 768], P('grp', 'seq'), parts along dimension 0
There are 2 independent parts, one for each index of `grp`. A program takes and returns all parts, laid end to end along the dimension named above; an argument that names none is the same for every part. Nothing has to cross between parts.
All inputs are finite; a program needn't handle non-finite values.
Results may differ from a plain program's by a relative error of at most 0.0051.
Values may be sent and summed in bfloat16 or wider, within the bound.
A program may use at most 192 MiB of HBM per device.

v0:
```python
import jax
import jax.numpy as jnp
from jax import lax
from jax.sharding import PartitionSpec as P


def rms_scale(values, gain):
    mean_square = jnp.mean(values * values, axis=-1, keepdims=True)
    return values * lax.rsqrt(mean_square + 1e-05) * gain


def second_section(columns, left_factor):
    mixed = jnp.einsum("jia,sajc->sijc", left_factor, columns, preferred_element_type=jnp.float32)
    return mixed.astype(jnp.bfloat16)


def body(
    tokens, right_factor, left_factor, twiddle, norm_gain, mix_gain, value_weight, gate_weight
):
    seqs_here, rows_here, width = tokens.shape
    blocks_here = right_factor.shape[0]
    block_len = right_factor.shape[1]
    widened = tokens.astype(jnp.float32)
    normed = rms_scale(widened, norm_gain).astype(jnp.bfloat16)
    blocked = normed.reshape(seqs_here, blocks_here, block_len, width)
    section_one = jnp.einsum(
        "ajb,sabc->sajc", right_factor, blocked, preferred_element_type=jnp.float32
    )
    section_one = (section_one * twiddle[None, :, :, None]).astype(jnp.bfloat16)
    columns = lax.all_to_all(section_one, "seq", split_axis=2, concat_axis=1, tiled=True)
    mixed_cols = second_section(columns, left_factor)
    mixed_back = lax.all_to_all(mixed_cols, "seq", split_axis=1, concat_axis=2, tiled=True)
    residual_sum = widened + mixed_back.reshape(seqs_here, rows_here, width).astype(jnp.float32)
    mix_normed = (
        rms_scale(residual_sum, mix_gain).astype(jnp.bfloat16).reshape(seqs_here * rows_here, width)
    )
    values_out = jnp.dot(mix_normed, value_weight, preferred_element_type=jnp.float32)
    gates = jnp.dot(mix_normed, gate_weight, preferred_element_type=jnp.float32)
    gated = (values_out * jax.nn.sigmoid(gates)).reshape(seqs_here, rows_here, width)
    return (residual_sum + gated).astype(jnp.bfloat16)


def solution(mesh):
    return jax.shard_map(
        body,
        mesh=mesh,
        in_specs=(
            P("grp", "seq", None),
            P("seq", None, None),
            P("seq", None, None),
            P("seq", None),
            P(),
            P(),
            P(),
            P(),
        ),
        out_specs=P("grp", "seq", None),
        check_vma=False,
    )
```

profile of v0, /device:TPU:1, one launch (start us, length us, event | category | flops | bytes accessed | tf_op | source)
XLA Modules:
  0.0 759.3 jit_solution(9899287681793575877)
XLA Ops:
  0.0 0.0 copy-start
  0.0 0.0 copy-start.2
  0.0 7.2 fusion
  7.2 0.0 copy-done.2
  7.3 0.0 copy-start.4
  7.3 11.8 %fusion.2 = bf16[1,8192,768]{2,1,0:T(8,128)(2,1)} fusion(bf16[1,8192,768]{2,1,0:T(8,128)(2,1)} %param.8, f32[768]{0:T(1024)S(1)} %copy-done.2, f32[8192]{0:T(1024)S(1)} %add_rsqrt_fusion.1), kind=kLoop, calls=%fused_computation.5 | loop fusion | flops 25165824 | bytes 25201664 | tf_op jit(solution)/shard_map/convert_element_type | solution.py:24
  19.1 0.0 copy-done.4
  19.1 16.0 %fusion.9 = bf16[1,16,512,768]{2,3,1,0:T(8,128)(2,1)} fusion(f32[16,512]{1,0:T(8,128)S(1)} %copy-done.4, bf16[16,512,768]{2,1,0:T(8,128)(2,1)} %bitcast.45, bf16[16,512,512]{2,1,0:T(8,128)(2,1)} %param.9), kind=kOutput, calls=%fused_computation.15 | convolution fusion | flops 6455033856 | bytes 33587200 | tf_op jit(solution)/shard_map/ajb,sabc->sajc/dot_general | solution.py:26
  35.1 17.6 %copy.19 = bf16[1,16,512,768]{3,1,0,2:T(8,128)(2,1)} copy(bf16[1,16,512,768]{2,3,1,0:T(8,128)(2,1)} %fusion.9) | data formatting | bytes 25165824 | tf_op jit(solution)/shard_map/convert_element_type | solution.py:29
  52.7 279.7 %all_to_all.24 = bf16[1,16,512,768]{3,1,0,2:T(8,128)(2,1)S(1)} all-to-all(bf16[1,16,512,768]{3,1,0,2:T(8,128)(2,1)} %copy.19), channel_id=1, replica_groups=mesh['grp'=2,'seq'=16] {'seq'}, dimensions={2} | all-to-all | bytes 25165824 | tf_op jit(solution)/shard_map/all_to_all | solution.py:30
  332.4 8.8 %copy.20 = bf16[1,16,512,768]{3,2,1,0:T(8,128)(2,1)S(1)} copy(bf16[1,16,512,768]{3,1,0,2:T(8,128)(2,1)S(1)} %all_to_all.24) | data formatting | bytes 25165824 | tf_op jit(solution)/shard_map/all_to_all | solution.py:30
  341.3 5.3 copy.21
  346.6 18.1 %convert_bitcast_fusion.1 = bf16[1,256,32,768]{1,3,2,0:T(8,128)(2,1)} fusion(bf16[32,256,256]{2,1,0:T(8,128)(2,1)} %param.10, bf16[256,32,768]{2,1,0:T(8,128)(2,1)} %bitcast.44), kind=kOutput, calls=%fused_computation.22 | convolution fusion | flops 3227516928 | bytes 29360128 | tf_op jit(solution)/shard_map/jia,sajc->sijc/dot_general | solution.py:13
  364.7 16.6 %copy.23 = bf16[1,256,32,768]{3,2,0,1:T(8,128)(2,1)} copy(bf16[1,256,32,768]{1,3,2,0:T(8,128)(2,1)} %convert_bitcast_fusion.1) | data formatting | bytes 25165824 | tf_op jit(solution)/shard_map/convert_element_type | solution.py:14
  381.3 278.1 %all_to_all.25 = bf16[1,256,32,768]{3,2,0,1:T(8,128)(2,1)S(1)} all-to-all(bf16[1,256,32,768]{3,2,0,1:T(8,128)(2,1)} %copy.23), channel_id=1, replica_groups=mesh['grp'=2,'seq'=16] {'seq'}, dimensions={1} | all-to-all | bytes 25165824 | tf_op jit(solution)/shard_map/all_to_all | solution.py:32
  659.4 0.0 slice-start
  659.4 0.0 slice-start.1
  659.4 10.6 %convert_bitcast_fusion = f32[1,16,16,32,768]{4,3,1,2,0:T(8,128)} fusion(bf16[1,16,16,32,768]{4,3,2,1,0:T(8,128)(2,1)S(1)} %bitcast.43), kind=kLoop, calls=%fused_computation.6 | loop fusion | flops 6291456 | bytes 37748736 | tf_op jit(solution)/shard_map/convert_element_type | solution.py:33
  670.0 0.0 slice-start.2
  670.0 18.3 %copy.25 = f32[1,16,16,32,768]{4,3,2,1,0:T(8,128)} copy(f32[1,16,16,32,768]{4,3,1,2,0:T(8,128)} %convert_bitcast_fusion) | data formatting | bytes 50331648 | tf_op jit(solution)/shard_map/convert_element_type | solution.py:33
  688.3 0.0 slice-done
  688.3 0.0 slice-done.1
  688.3 0.0 slice-done.2
  688.3 0.0 copy-start.5
  688.3 17.8 %multiply_reduce_fusion = (f32[8192]{0:T(1024)S(1)}, f32[1,8192,768]{2,1,0:T(8,128)}) fusion(f32[1,16,16,32,768]{4,3,2,1,0:T(8,128)} %copy.25, bf16[1,8192,768]{2,1,0:T(8,128)(2,1)S(1)} %bitcast.41), kind=kLoop, calls=%fused_computation.12 | loop fusion | flops 25157632 | bytes 62947328 | tf_op jit(solution)/shard_map/reduce_sum | solution.py:8
  706.1 0.0 copy-done
  706.1 0.0 copy-done.5
  706.1 0.0 copy-start.3
  706.1 19.5 %fusion.7 = f32[8192,768]{1,0:T(8,128)} fusion(bf16[768,768]{1,0:T(8,128)(2,1)S(1)} %copy-done, f32[1,8192,768]{2,1,0:T(8,128)} %get-tuple-element.6, f32[768]{0:T(1024)S(1)} %copy-done.5, f32[8192]{0:T(1024)S(1)} %add_rsqrt_fusion), kind=kOutput, calls=%fused_computation.14 | convolution fusion | flops 9682550784 | bytes 51547136 | tf_op jit(solution)/shard_map/dot_general | solution.py:37
  725.6 0.0 copy-done.3
  725.6 0.0 copy-start.1
  725.6 33.6 %fusion.3 = bf16[1,8192,768]{2,1,0:T(8,128)(2,1)} fusion(f32[1,8192,768]{2,1,0:T(8,128)} %get-tuple-element.6, f32[8192,768]{1,0:T(8,128)} %fusion.7, bf16[768,768]{1,0:T(8,128)(2,1)S(1)} %copy-done.3, f32[768]{0:T(1024)S(1)} %copy-done.5, f32[8192]{0:T(1024)S(1)} %add_rsqrt_fusion), kind=kOutput, calls=%fused_computation.8 | convolution fusion | flops 9720299520 | bytes 64130048 | tf_op jit(solution)/shard_map/dot_general | solution.py:38
  759.3 0.0 copy-done.1
  (3 shorter events, 0.0 us)
Async XLA Ops:
  0.0 706.1 %copy-start = (bf16[768,768]{1,0:T(8,128)(2,1)S(1)}, bf16[768,768]{1,0:T(8,128)(2,1)}, u32[]{:S(2)}) copy-start(bf16[768,768]{1,0:T(8,128)(2,1)} %param.14) | copy-start | bytes 3538948
  0.0 7.2 copy-start.2
  7.3 11.8 %copy-start.4 = (f32[16,512]{1,0:T(8,128)S(1)}, f32[16,512]{1,0:T(8,128)}, u32[]{:S(2)}) copy-start(f32[16,512]{1,0:T(8,128)} %param.11) | copy-start | bytes 98308
  659.4 28.9 %slice-start = ((s8[12582912]{0:T(1024)(128)(4,1)}), s8[4194304]{0:T(1024)(128)(4,1)S(1)}, s32[]{:S(2)}) async-start(s8[12582912]{0:T(1024)(128)(4,1)} %bitcast.40), calls=%async_computation.2 | async-start | bytes 8388608
  659.4 28.9 %slice-start.1 = ((s8[12582912]{0:T(1024)(128)(4,1)}), s8[4194304]{0:T(1024)(128)(4,1)S(1)}, s32[]{:S(2)}) async-start(s8[12582912]{0:T(1024)(128)(4,1)} %bitcast.40), calls=%async_computation.3 | async-start | bytes 8388608
  670.0 18.3 %slice-start.2 = ((s8[12582912]{0:T(1024)(128)(4,1)}), s8[4194304]{0:T(1024)(128)(4,1)S(1)}, s32[]{:S(2)}) async-start(s8[12582912]{0:T(1024)(128)(4,1)} %bitcast.40), calls=%async_computation.4 | async-start | bytes 8388608
  688.3 17.8 %copy-start.5 = (f32[768]{0:T(1024)S(1)}, f32[768]{0:T(1024)}, u32[]{:S(2)}) copy-start(f32[768]{0:T(1024)} %param.13) | copy-start | bytes 9220
  706.1 19.5 %copy-start.3 = (bf16[768,768]{1,0:T(8,128)(2,1)S(1)}, bf16[768,768]{1,0:T(8,128)(2,1)}, u32[]{:S(2)}) copy-start(bf16[768,768]{1,0:T(8,128)(2,1)} %param.15) | copy-start | bytes 3538948
  725.6 33.6 %copy-start.1 = (bf16[768,768]{1,0:T(8,128)(2,1)S(1)}, bf16[768,768]{1,0:T(8,128)(2,1)}, u32[]{:S(2)}) copy-start(bf16[768,768]{1,0:T(8,128)(2,1)} %param.14) | copy-start | bytes 3538948
where the time goes:
time: 760 us; the launch traced here: 759 us
  blocking collectives  558 us (73%)
  matrix products  87.2 us (11%)
  local copies, waits for them, and re-layouts  66.6 us (9%)
  other arithmetic  47.4 us (6%)
    all_to_all x1, blocking collectives, body(): lax.all_to_all(section_one, 'seq', split_axis=2, concat_axis=1, tiled=True)  280 us
    all_to_all x1, blocking collectives, body(): lax.all_to_all(mixed_cols, 'seq', split_axis=1, concat_axis=2, tiled=True)  278 us
    dot_general x1, matrix products, body(): gates = jnp.dot(mix_normed, gate_weight, preferred_element_type=jnp.float32)  33.6 us
    reduce_sum x2, other arithmetic, rms_scale(): mean_square = jnp.mean(values * values, axis=-1, keepdims=True)  25 us
    dot_general x1, matrix products, body(): jnp.dot(mix_normed, value_weight, preferred_element_type=jnp.float32)  19.5 us
    convert_element_type x1, local copies, waits for them, and re-layouts, body(): mixed_back.reshape(seqs_here, rows_here, width).astype(jnp.float32)  18.3 us
    dot_general x1, matrix products, second_section(): jnp.einsum('jia,sajc->sijc', left_factor, columns, preferred_element_type...  18.1 us
    convert_element_type x1, local copies, waits for them, and re-layouts, body(): section_one = (section_one * twiddle[None, :, :, None]).astype(jnp.bfloat16)  17.6 us

commit v1 on v0

--- a/solution.py
+++ b/solution.py
@@ -1,7 +1,32 @@
+import functools
 import jax
 import jax.numpy as jnp
 from jax import lax
 from jax.sharding import PartitionSpec as P
+from jax.lax import axis_index, axis_size, ppermute
+
+
+def _point_links(vec, join_dim, pos_dim):
+    y1, small = (axis_size("seq"), axis_index("seq"))
+    e_now = vec.shape[join_dim] // y1
+    x_now = list(vec.shape)
+    x_now[join_dim] = e_now
+    s_next = x_now[pos_dim]
+    x_now[pos_dim] = s_next * y1
+    b = 0
+    reached = jnp.zeros(x_now, vec.dtype)
+    while b < y1:
+        outer = lax.dynamic_slice_in_dim(vec, (small ^ b) * e_now, e_now, axis=join_dim)
+        if b:
+            outer = ppermute(outer, "seq", [(p, p ^ b) for p in range(y1)])
+        reached = lax.dynamic_update_slice_in_dim(
+            reached, outer, (small ^ b) * s_next, axis=pos_dim
+        )
+        b = b + 1
+    return reached
+
+
+shape_the_wall = functools.partial(_point_links, join_dim=1, pos_dim=2)
 
 
 def rms_scale(values, gain):
@@ -29,7 +54,7 @@
     section_one = (section_one * twiddle[None, :, :, None]).astype(jnp.bfloat16)
     columns = lax.all_to_all(section_one, "seq", split_axis=2, concat_axis=1, tiled=True)
     mixed_cols = second_section(columns, left_factor)
-    mixed_back = lax.all_to_all(mixed_cols, "seq", split_axis=1, concat_axis=2, tiled=True)
+    mixed_back = shape_the_wall(mixed_cols)
     residual_sum = widened + mixed_back.reshape(seqs_here, rows_here, width).astype(jnp.float32)
     mix_normed = (
         rms_scale(residual_sum, mix_gain).astype(jnp.bfloat16).reshape(seqs_here * rows_here, width)

time: 760 us -> 751 us (0.988)
  the two profiles are of different devices: /device:TPU:1 before, /device:TPU:13 now
where the time goes in v1:
time: 751 us; the launch traced here: 750 us
  waiting for transfers between devices  497 us (66%)
  matrix products  90 us (12%)
  local copies, waits for them, and re-layouts  86.4 us (12%)
  starting transfers between devices  49 us (7%)
  other arithmetic  27.3 us (4%)
    all_to_all x1, waiting for transfers between devices, body(): lax.all_to_all(section_one, 'seq', split_axis=2, concat_axis=1, tiled=True)  272 us
    ppermute x15, waiting for transfers between devices, _point_links(): outer = ppermute(outer, 'seq', [(p, p ^ b) for p in range(y1)])  225 us
    ppermute x15, starting transfers between devices, _point_links(): outer = ppermute(outer, 'seq', [(p, p ^ b) for p in range(y1)])  42.4 us
    dot_general x1, matrix products, body(): gates = jnp.dot(mix_normed, gate_weight, preferred_element_type=jnp.float32)  38.6 us
    all_to_all x2, local copies, waits for them, and re-layouts, body(): lax.all_to_all(section_one, 'seq', split_axis=2, concat_axis=1, tiled=True)  29.6 us
    dynamic_update_slice x16, local copies, waits for them, and re-layouts, _point_links(): lax.dynamic_update_slice_in_dim(reached, outer, (small ^ b) * s_next, axi...  24.5 us
    dot_general x1, matrix products, body(): jnp.dot(mix_normed, value_weight, preferred_element_type=jnp.float32)  21.4 us
    convert_element_type x1, local copies, waits for them, and re-layouts, body(): section_one = (section_one * twiddle[None, :, :, None]).astype(jnp.bfloat16)  17.6 us
  transfers between devices with their start and end apart: 16, of which 11 were waited for; matrix products, arithmetic and copies ran while one was open for 4% of the time, Pallas kernels for 0%

profile of v1, /device:TPU:13, one launch (start us, length us, event | category | flops | bytes accessed | tf_op | source)
XLA Modules:
  0.0 750.2 jit_solution(7188614443723958596)
XLA Ops:
  0.0 0.0 copy-start
  0.0 7.2 fusion
  7.3 0.0 copy-start.8
  7.3 11.8 %fusion.2 = bf16[1,8192,768]{2,1,0:T(8,128)(2,1)} fusion(bf16[1,8192,768]{2,1,0:T(8,128)(2,1)} %param.8, f32[768]{0:T(1024)S(1)} %copy-done.6, f32[8192]{0:T(1024)S(1)} %add_rsqrt_fusion.1), kind=kLoop, calls=%fused_computation.5 | loop fusion | flops 25165824 | bytes 25201664 | tf_op jit(solution)/shard_map/convert_element_type | solution.py:49
  19.1 16.2 %fusion.9 = bf16[1,16,512,768]{2,3,1,0:T(8,128)(2,1)} fusion(f32[16,512]{1,0:T(8,128)S(1)} %copy-done.8, bf16[16,512,768]{2,1,0:T(8,128)(2,1)} %bitcast.100, bf16[16,512,512]{2,1,0:T(8,128)(2,1)} %param.9), kind=kOutput, calls=%fused_computation.14 | convolution fusion | flops 6455033856 | bytes 33587200 | tf_op jit(solution)/shard_map/ajb,sabc->sajc/dot_general | solution.py:51
  35.3 17.6 %copy.31 = bf16[1,16,512,768]{3,1,0,2:T(8,128)(2,1)} copy(bf16[1,16,512,768]{2,3,1,0:T(8,128)(2,1)} %fusion.9) | data formatting | bytes 25165824 | tf_op jit(solution)/shard_map/convert_element_type | solution.py:54
  52.9 6.6 all-to-all-start
  59.4 272.2 %all-to-all-done = bf16[1,16,512,768]{3,1,0,2:T(8,128)(2,1)} async-done(((bf16[1,16,512,768]{3,1,0,2:T(8,128)(2,1)}), bf16[1,16,512,768]{3,1,0,2:T(8,128)(2,1)}, u32[]{:S(2)}, u32[]{:S(2)}) %all-to-all-start) | async-done | bytes 12582944 | tf_op jit(solution)/shard_map/all_to_all | solution.py:55
  331.6 7.9 %copy.32 = bf16[1,16,512,768]{3,2,1,0:T(8,128)(2,1)S(1)} copy(bf16[1,16,512,768]{3,1,0,2:T(8,128)(2,1)} %all-to-all-done) | data formatting | bytes 25165824 | tf_op jit(solution)/shard_map/all_to_all | solution.py:55
  339.6 21.7 %copy.33 = bf16[1,16,16,32,768]{4,2,1,3,0:T(8,128)(2,1)} copy(bf16[1,16,16,32,768]{4,3,1,2,0:T(8,128)(2,1)S(1)} %bitcast.99) | data formatting | bytes 25165824 | tf_op jit(solution)/shard_map/all_to_all | solution.py:55
  361.3 13.8 %convolution_convert_fusion = bf16[32,768,256]{1,2,0:T(8,128)(2,1)} fusion(bf16[32,256,256]{2,1,0:T(8,128)(2,1)} %param.10, bf16[256,32,768]{2,0,1:T(8,128)(2,1)} %bitcast.96), kind=kOutput, calls=%fused_computation.19 | convolution fusion | flops 3227516928 | bytes 29360128 | tf_op jit(solution)/shard_map/jia,sajc->sijc/dot_general | solution.py:38
  375.1 8.8 %dynamic-slice_bitcast_fusion = (bf16[1,16,32,768]{3,1,0,2:T(8,128)(2,1)S(1)}, bf16[1,16,32,768]{3,1,0,2:T(8,128)(2,1)S(1)}, bf16[1,16,32,768]{3,1,0,2:T(8,128)(...) fusion(bf16[32,768,256]{1,2,0:T(8,128)(2,1)} %convolution_conve, ...), kind=kLoop, calls=%fused_computation.36 | loop fusion | bytes 25165888 | tf_op jit(solution)/shard_map/dynamic_slice | solution.py:19
  383.9 0.3 collective-permute-start
  384.2 0.0 collective-permute-start.1
  384.2 1.7 collective-permute-start.14
  385.9 0.8 collective-permute-start.13
  386.7 1.8 collective-permute-start.2
  388.6 5.8 broadcast_in_dim.2
  394.4 1.2 copy_dynamic-update-slice_fusion.15
  395.6 0.0 collective-permute-done
  395.6 0.0 collective-permute-start.3
  395.6 2.7 copy_dynamic-update-slice_fusion.14
  398.3 5.3 collective-permute-done.1
  403.5 0.0 collective-permute-start.4
  403.5 2.3 copy_dynamic-update-slice_fusion.13
  405.8 15.3 %collective-permute-done.2 = bf16[1,16,32,768]{3,1,0,2:T(8,128)(2,1)} collective-permute-done((bf16[1,16,32,768]{3,1,0,2:T(8,128)(2,1)}, bf16[1,16,32,768]{3,1,0,2:T(8,128)(2,1)}, u32[]{:S(2)}, u32[]{:S(2)}) %collective-permute-start.2) | collective-permute-done | bytes 786464 | tf_op jit(solution)/shard_map/ppermute | solution.py:21
  421.1 18.2 %collective-permute-start.5 = (bf16[1,16,32,768]{3,1,0,2:T(8,128)(2,1)}, bf16[1,16,32,768]{3,1,0,2:T(8,128)(2,1)S(1)}, u32[]{:S(2)}, u32[]{:S(2)}) collective-permute-start(bf16[1,16,32,768]{3,1,0,2:T(8,128)(2,1)} %get-tuple-element.14), channel_id=1, source_target_pairs={{0,6},{1,7},{2,4},{3,5},{4,2},{5,3},{6,0},{7,1},{8,14},{9,15},{10,... | collective-permute-start | bytes 2359304 | tf_op jit(solution)/shard_map/ppermute | solution.py:21
  439.3 2.3 copy_dynamic-update-slice_fusion.12
  441.6 0.0 collective-permute-done.3
  441.6 0.3 collective-permute-start.6
  441.9 1.1 copy_dynamic-update-slice_fusion.11
  443.0 14.0 %collective-permute-done.4 = bf16[1,16,32,768]{3,1,0,2:T(8,128)(2,1)S(1)} collective-permute-done((bf16[1,16,32,768]{3,1,0,2:T(8,128)(2,1)}, bf16[1,16,32,768]{3,1,0,2:T(8,128)(2,1)S(1)}, u32[]{:S(2)}, u32[]{:S(2)}) %collective-permute-start.4) | collective-permute-done | bytes 786464 | tf_op jit(solution)/shard_map/ppermute | solution.py:21
  457.0 4.4 collective-permute-start.7
  461.4 1.1 copy_dynamic-update-slice_fusion.10
  462.5 24.4 %collective-permute-done.5 = bf16[1,16,32,768]{3,1,0,2:T(8,128)(2,1)S(1)} collective-permute-done((bf16[1,16,32,768]{3,1,0,2:T(8,128)(2,1)}, bf16[1,16,32,768]{3,1,0,2:T(8,128)(2,1)S(1)}, u32[]{:S(2)}, u32[]{:S(2)}) %collective-permute-start.5) | collective-permute-done | bytes 786464 | tf_op jit(solution)/shard_map/ppermute | solution.py:21
  486.9 6.8 collective-permute-start.8
  493.7 1.1 copy_dynamic-update-slice_fusion.9
  494.8 9.0 %collective-permute-done.6 = bf16[1,16,32,768]{3,1,0,2:T(8,128)(2,1)S(1)} collective-permute-done((bf16[1,16,32,768]{3,1,0,2:T(8,128)(2,1)}, bf16[1,16,32,768]{3,1,0,2:T(8,128)(2,1)S(1)}, u32[]{:S(2)}, u32[]{:S(2)}) %collective-permute-start.6) | collective-permute-done | bytes 786464 | tf_op jit(solution)/shard_map/ppermute | solution.py:21
  503.8 6.6 collective-permute-start.9
  510.5 1.2 copy_dynamic-update-slice_fusion.8
  511.7 0.0 collective-permute-done.7
  511.7 0.3 collective-permute-start.10
  512.0 1.1 copy_dynamic-update-slice_fusion.7
  513.1 60.8 %collective-permute-done.8 = bf16[1,16,32,768]{3,1,0,2:T(8,128)(2,1)S(1)} collective-permute-done((bf16[1,16,32,768]{3,1,0,2:T(8,128)(2,1)}, bf16[1,16,32,768]{3,1,0,2:T(8,128)(2,1)S(1)}, u32[]{:S(2)}, u32[]{:S(2)}) %collective-permute-start.8) | collective-permute-done | bytes 786464 | tf_op jit(solution)/shard_map/ppermute | solution.py:21
  574.0 0.4 collective-permute-start.11
  574.4 1.1 copy_dynamic-update-slice_fusion.6
  575.5 32.0 %collective-permute-done.9 = bf16[1,16,32,768]{3,1,0,2:T(8,128)(2,1)S(1)} collective-permute-done((bf16[1,16,32,768]{3,1,0,2:T(8,128)(2,1)S(1)}, bf16[1,16,32,768]{3,1,0,2:T(8,128)(2,1)S(1)}, u32[]{:S(2)}, u32[]{:S(2)}) %collective-permute-start.9) | collective-permute-done | bytes 786464 | tf_op jit(solution)/shard_map/ppermute | solution.py:21
  607.6 0.7 collective-permute-start.12
  608.3 1.1 copy_dynamic-update-slice_fusion.5
  609.4 31.9 %collective-permute-done.10 = bf16[1,16,32,768]{3,1,0,2:T(8,128)(2,1)S(1)} collective-permute-done((bf16[1,16,32,768]{3,1,0,2:T(8,128)(2,1)S(1)}, bf16[1,16,32,768]{3,1,0,2:T(8,128)(2,1)S(1)}, u32[]{:S(2)}, u32[]{:S(2)}) %collective-permute-start.10) | collective-permute-done | bytes 786464 | tf_op jit(solution)/shard_map/ppermute | solution.py:21
  641.3 1.2 copy_dynamic-update-slice_fusion.4
  642.5 16.8 %collective-permute-done.11 = bf16[1,16,32,768]{3,1,0,2:T(8,128)(2,1)S(1)} collective-permute-done((bf16[1,16,32,768]{3,1,0,2:T(8,128)(2,1)S(1)}, bf16[1,16,32,768]{3,1,0,2:T(8,128)(2,1)S(1)}, u32[]{:S(2)}, u32[]{:S(2)}) %collective-permute-start.11) | collective-permute-done | bytes 786464 | tf_op jit(solution)/shard_map/ppermute | solution.py:21
  659.3 1.1 copy_dynamic-update-slice_fusion.3
  660.4 15.7 %collective-permute-done.12 = bf16[1,16,32,768]{3,1,0,2:T(8,128)(2,1)S(1)} collective-permute-done((bf16[1,16,32,768]{3,1,0,2:T(8,128)(2,1)S(1)}, bf16[1,16,32,768]{3,1,0,2:T(8,128)(2,1)S(1)}, u32[]{:S(2)}, u32[]{:S(2)}) %collective-permute-start.12) | collective-permute-done | bytes 786464 | tf_op jit(solution)/shard_map/ppermute | solution.py:21
  676.1 1.1 copy_dynamic-update-slice_fusion.2
  677.3 0.0 collective-permute-done.13
  677.3 2.3 copy_dynamic-update-slice_fusion.1
  679.5 0.0 collective-permute-done.14
  679.5 2.3 copy_dynamic-update-slice_fusion
  681.9 0.0 copy-start.9
  681.9 8.2 %multiply_reduce_fusion = f32[8192]{0:T(1024)S(1)} fusion(bf16[1,8192,768]{2,1,0:T(8,128)(2,1)S(1)} %bitcast.95, bf16[1,16,512,768]{3,2,1,0:T(8,128)(2,1)} %copy_dynamic-update-slice_fusion), kind=kLoop, calls=%fused_computation.11 | loop fusion | flops 31449088 | bytes 25198592 | tf_op jit(solution)/shard_map/reduce_sum | solution.py:33
  690.2 0.0 copy-start.7
  690.2 21.4 %fusion.7 = f32[8192,768]{1,0:T(8,128)} fusion(bf16[768,768]{1,0:T(8,128)(2,1)S(1)} %copy-done, bf16[1,8192,768]{2,1,0:T(8,128)(2,1)} %bitcast.97, bf16[1,8192,768]{2,1,0:T(8,128)(2,1)} %param.8, f32[768]{0:T(1024)S(1)} %copy-done.9, f32[8192]{0:T(1024)S(1)} %add_rsqrt_fusion), kind=kOutput, calls=%fused_computation.13 | convolution fusion | flops 9701425152 | bytes 51547136 | tf_op jit(solution)/shard_map/dot_general | solution.py:62
  711.6 38.6 %fusion.3 = bf16[1,8192,768]{2,1,0:T(8,128)(2,1)} fusion(f32[8192,768]{1,0:T(8,128)} %fusion.7, bf16[1,8192,768]{2,1,0:T(8,128)(2,1)} %bitcast.98, bf16[1,8192,768]{2,1,0:T(8,128)(2,1)} %param.8, bf16[768,768]{1,0:T(8,128)(2,1)S(1)} %copy-done.7, f32[768]{0:T(1024)S(1)} %copy-done.9, f32[8192]{0:T(1024)S(1)} %add_rsqrt_fusion), kind=kOutput, calls=%fused_computation.7 | convolution fusion | flops 9758048256 | bytes 64130048 | tf_op jit(solution)/shard_map/dot_general | solution.py:63
  (25 shorter events, 0.1 us)
Async XLA Ops:
  0.0 690.2 %copy-start = (bf16[768,768]{1,0:T(8,128)(2,1)S(1)}, bf16[768,768]{1,0:T(8,128)(2,1)}, u32[]{:S(2)}) copy-start(bf16[768,768]{1,0:T(8,128)(2,1)} %param.14) | copy-start | bytes 3538948
  0.0 7.2 copy-start.6
  7.3 11.8 %copy-start.8 = (f32[16,512]{1,0:T(8,128)S(1)}, f32[16,512]{1,0:T(8,128)}, u32[]{:S(2)}) copy-start(f32[16,512]{1,0:T(8,128)} %param.11) | copy-start | bytes 98308
  52.9 278.8 %all-to-all-start = ((bf16[1,16,512,768]{3,1,0,2:T(8,128)(2,1)}), bf16[1,16,512,768]{3,1,0,2:T(8,128)(2,1)}, u32[]{:S(2)}, u32[]{:S(2)}) async-start(bf16[1,16,512,768]{3,1,0,2:T(8,128)(2,1)} %copy.31), calls=%async_computation | async-start | bytes 25165824 | tf_op jit(solution)/shard_map/all_to_all | solution.py:55
  383.9 11.7 %collective-permute-start = (bf16[1,16,32,768]{3,1,0,2:T(8,128)(2,1)}, bf16[1,16,32,768]{3,1,0,2:T(8,128)(2,1)}, u32[]{:S(2)}, u32[]{:S(2)}) collective-permute-start(bf16[1,16,32,768]{3,1,0,2:T(8,128)(2,1)} %get-tuple-element.19), channel_id=1, source_target_pairs={{0,1},{1,0},{2,3},{3,2},{4,5},{5,4},{6,7},{7,6},{8,9},{9,8},{10,11... | collective-permute-start | bytes 2359304 | tf_op jit(solution)/shard_map/ppermute | solution.py:21
  384.2 19.3 %collective-permute-start.1 = (bf16[1,16,32,768]{3,1,0,2:T(8,128)(2,1)}, bf16[1,16,32,768]{3,1,0,2:T(8,128)(2,1)}, u32[]{:S(2)}, u32[]{:S(2)}) collective-permute-start(bf16[1,16,32,768]{3,1,0,2:T(8,128)(2,1)} %get-tuple-element.18), channel_id=1, source_target_pairs={{0,2},{1,3},{2,0},{3,1},{4,6},{5,7},{6,4},{7,5},{8,10},{9,11},{10,... | collective-permute-start | bytes 2359304 | tf_op jit(solution)/shard_map/ppermute | solution.py:21
  384.2 119.6 %copy-start.5 = (bf16[1,16,32,768]{3,1,0,2:T(8,128)(2,1)S(1)}, bf16[1,16,32,768]{3,1,0,2:T(8,128)(2,1)}, u32[]{:S(2)}) copy-start(bf16[1,16,32,768]{3,1,0,2:T(8,128)(2,1)} %get-tuple-element.10) | copy-start | bytes 2359300
  384.2 295.3 %collective-permute-start.14 = (bf16[1,16,32,768]{3,1,0,2:T(8,128)(2,1)S(1)}, bf16[1,16,32,768]{3,1,0,2:T(8,128)(2,1)}, u32[]{:S(2)}, u32[]{:S(2)}) collective-permute-start(bf16[1,16,32,768]{3,1,0,2:T(8,128)(2,1)S(1)} %get-tuple-element.5), channel_id=1, source_target_pairs={{0,15},{1,14},{2,13},{3,12},{4,11},{5,10},{6,9},{7,8},{8,7},{9,6},... | collective-permute-start | bytes 2359304 | tf_op jit(solution)/shard_map/ppermute | solution.py:21
  385.9 291.4 %collective-permute-start.13 = (bf16[1,16,32,768]{3,1,0,2:T(8,128)(2,1)S(1)}, bf16[1,16,32,768]{3,1,0,2:T(8,128)(2,1)}, u32[]{:S(2)}, u32[]{:S(2)}) collective-permute-start(bf16[1,16,32,768]{3,1,0,2:T(8,128)(2,1)S(1)} %get-tuple-element.6), channel_id=1, source_target_pairs={{0,14},{1,15},{2,12},{3,13},{4,10},{5,11},{6,8},{7,9},{8,6},{9,7},... | collective-permute-start | bytes 2359304 | tf_op jit(solution)/shard_map/ppermute | solution.py:21
  386.7 34.4 %collective-permute-start.2 = (bf16[1,16,32,768]{3,1,0,2:T(8,128)(2,1)}, bf16[1,16,32,768]{3,1,0,2:T(8,128)(2,1)}, u32[]{:S(2)}, u32[]{:S(2)}) collective-permute-start(bf16[1,16,32,768]{3,1,0,2:T(8,128)(2,1)} %get-tuple-element.17), channel_id=1, source_target_pairs={{0,3},{1,2},{2,1},{3,0},{4,7},{5,6},{6,5},{7,4},{8,11},{9,10},{10,... | collective-permute-start | bytes 2359304 | tf_op jit(solution)/shard_map/ppermute | solution.py:21
  388.6 123.1 %copy-start.4 = (bf16[1,16,32,768]{3,1,0,2:T(8,128)(2,1)S(1)}, bf16[1,16,32,768]{3,1,0,2:T(8,128)(2,1)}, u32[]{:S(2)}) copy-start(bf16[1,16,32,768]{3,1,0,2:T(8,128)(2,1)} %get-tuple-element.9) | copy-start | bytes 2359300
  388.6 185.4 %copy-start.3 = (bf16[1,16,32,768]{3,1,0,2:T(8,128)(2,1)S(1)}, bf16[1,16,32,768]{3,1,0,2:T(8,128)(2,1)}, u32[]{:S(2)}) copy-start(bf16[1,16,32,768]{3,1,0,2:T(8,128)(2,1)} %get-tuple-element.8) | copy-start | bytes 2359300
  388.6 219.0 %copy-start.2 = (bf16[1,16,32,768]{3,1,0,2:T(8,128)(2,1)S(1)}, bf16[1,16,32,768]{3,1,0,2:T(8,128)(2,1)}, u32[]{:S(2)}) copy-start(bf16[1,16,32,768]{3,1,0,2:T(8,128)(2,1)} %get-tuple-element.7) | copy-start | bytes 2359300
  394.4 287.5 %slice-start = ((s8[12582912]{0:T(1024)(128)(4,1)}), s8[4194304]{0:T(1024)(128)(4,1)S(1)}, s32[]{:S(2)}) async-start(s8[12582912]{0:T(1024)(128)(4,1)} %bitcast.94), calls=%async_computation.1 | async-start | bytes 8388608
  395.6 46.0 %collective-permute-start.3 = (bf16[1,16,32,768]{3,1,0,2:T(8,128)(2,1)}, bf16[1,16,32,768]{3,1,0,2:T(8,128)(2,1)S(1)}, u32[]{:S(2)}, u32[]{:S(2)}) collective-permute-start(bf16[1,16,32,768]{3,1,0,2:T(8,128)(2,1)} %get-tuple-element.16), channel_id=1, source_target_pairs={{0,4},{1,5},{2,6},{3,7},{4,0},{5,1},{6,2},{7,3},{8,12},{9,13},{10,... | collective-permute-start | bytes 2359304 | tf_op jit(solution)/shard_map/ppermute | solution.py:21
  403.5 53.5 %collective-permute-start.4 = (bf16[1,16,32,768]{3,1,0,2:T(8,128)(2,1)}, bf16[1,16,32,768]{3,1,0,2:T(8,128)(2,1)S(1)}, u32[]{:S(2)}, u32[]{:S(2)}) collective-permute-start(bf16[1,16,32,768]{3,1,0,2:T(8,128)(2,1)} %get-tuple-element.15), channel_id=1, source_target_pairs={{0,5},{1,4},{2,7},{3,6},{4,1},{5,0},{6,3},{7,2},{8,13},{9,12},{10,... | collective-permute-start | bytes 2359304 | tf_op jit(solution)/shard_map/ppermute | solution.py:21
  421.1 65.7 %collective-permute-start.5 = (bf16[1,16,32,768]{3,1,0,2:T(8,128)(2,1)}, bf16[1,16,32,768]{3,1,0,2:T(8,128)(2,1)S(1)}, u32[]{:S(2)}, u32[]{:S(2)}) collective-permute-start(bf16[1,16,32,768]{3,1,0,2:T(8,128)(2,1)} %get-tuple-element.14), channel_id=1, source_target_pairs={{0,6},{1,7},{2,4},{3,5},{4,2},{5,3},{6,0},{7,1},{8,14},{9,15},{10,... | collective-permute-start | bytes 2359304 | tf_op jit(solution)/shard_map/ppermute | solution.py:21
  441.6 62.2 %collective-permute-start.6 = (bf16[1,16,32,768]{3,1,0,2:T(8,128)(2,1)}, bf16[1,16,32,768]{3,1,0,2:T(8,128)(2,1)S(1)}, u32[]{:S(2)}, u32[]{:S(2)}) collective-permute-start(bf16[1,16,32,768]{3,1,0,2:T(8,128)(2,1)} %get-tuple-element.13), channel_id=1, source_target_pairs={{0,7},{1,6},{2,5},{3,4},{4,3},{5,2},{6,1},{7,0},{8,15},{9,14},{10,... | collective-permute-start | bytes 2359304 | tf_op jit(solution)/shard_map/ppermute | solution.py:21
  457.0 224.9 %slice-start.1 = ((s8[12582912]{0:T(1024)(128)(4,1)}), s8[4194304]{0:T(1024)(128)(4,1)S(1)}, s32[]{:S(2)}) async-start(s8[12582912]{0:T(1024)(128)(4,1)} %bitcast.94), calls=%async_computation.2 | async-start | bytes 8388608
  457.0 54.7 %collective-permute-start.7 = (bf16[1,16,32,768]{3,1,0,2:T(8,128)(2,1)}, bf16[1,16,32,768]{3,1,0,2:T(8,128)(2,1)S(1)}, u32[]{:S(2)}, u32[]{:S(2)}) collective-permute-start(bf16[1,16,32,768]{3,1,0,2:T(8,128)(2,1)} %get-tuple-element.12), channel_id=1, source_target_pairs={{0,8},{1,9},{2,10},{3,11},{4,12},{5,13},{6,14},{7,15},{8,0},{9,1},... | collective-permute-start | bytes 2359304 | tf_op jit(solution)/shard_map/ppermute | solution.py:21
  486.9 87.1 %collective-permute-start.8 = (bf16[1,16,32,768]{3,1,0,2:T(8,128)(2,1)}, bf16[1,16,32,768]{3,1,0,2:T(8,128)(2,1)S(1)}, u32[]{:S(2)}, u32[]{:S(2)}) collective-permute-start(bf16[1,16,32,768]{3,1,0,2:T(8,128)(2,1)} %get-tuple-element.11), channel_id=1, source_target_pairs={{0,9},{1,8},{2,11},{3,10},{4,13},{5,12},{6,15},{7,14},{8,1},{9,0},... | collective-permute-start | bytes 2359304 | tf_op jit(solution)/shard_map/ppermute | solution.py:21
  503.8 103.7 %collective-permute-start.9 = (bf16[1,16,32,768]{3,1,0,2:T(8,128)(2,1)S(1)}, bf16[1,16,32,768]{3,1,0,2:T(8,128)(2,1)S(1)}, u32[]{:S(2)}, u32[]{:S(2)}) collective-permute-start(bf16[1,16,32,768]{3,1,0,2:T(8,128)(2,1)S(1)} %copy-done.5), channel_id=1, source_target_pairs={{0,10},{1,11},{2,8},{3,9},{4,14},{5,15},{6,12},{7,13},{8,2},{9,3},... | collective-permute-start | bytes 2359304 | tf_op jit(solution)/shard_map/ppermute | solution.py:21
  511.7 129.6 %collective-permute-start.10 = (bf16[1,16,32,768]{3,1,0,2:T(8,128)(2,1)S(1)}, bf16[1,16,32,768]{3,1,0,2:T(8,128)(2,1)S(1)}, u32[]{:S(2)}, u32[]{:S(2)}) collective-permute-start(bf16[1,16,32,768]{3,1,0,2:T(8,128)(2,1)S(1)} %copy-done.4), channel_id=1, source_target_pairs={{0,11},{1,10},{2,9},{3,8},{4,15},{5,14},{6,13},{7,12},{8,3},{9,2},... | collective-permute-start | bytes 2359304 | tf_op jit(solution)/shard_map/ppermute | solution.py:21
  574.0 85.3 %collective-permute-start.11 = (bf16[1,16,32,768]{3,1,0,2:T(8,128)(2,1)S(1)}, bf16[1,16,32,768]{3,1,0,2:T(8,128)(2,1)S(1)}, u32[]{:S(2)}, u32[]{:S(2)}) collective-permute-start(bf16[1,16,32,768]{3,1,0,2:T(8,128)(2,1)S(1)} %copy-done.3), channel_id=1, source_target_pairs={{0,12},{1,13},{2,14},{3,15},{4,8},{5,9},{6,10},{7,11},{8,4},{9,5},... | collective-permute-start | bytes 2359304 | tf_op jit(solution)/shard_map/ppermute | solution.py:21
  607.6 74.3 %slice-start.2 = ((s8[12582912]{0:T(1024)(128)(4,1)}), s8[4194304]{0:T(1024)(128)(4,1)S(1)}, s32[]{:S(2)}) async-start(s8[12582912]{0:T(1024)(128)(4,1)} %bitcast.94), calls=%async_computation.3 | async-start | bytes 8388608
  607.6 68.6 %collective-permute-start.12 = (bf16[1,16,32,768]{3,1,0,2:T(8,128)(2,1)S(1)}, bf16[1,16,32,768]{3,1,0,2:T(8,128)(2,1)S(1)}, u32[]{:S(2)}, u32[]{:S(2)}) collective-permute-start(bf16[1,16,32,768]{3,1,0,2:T(8,128)(2,1)S(1)} %copy-done.2), channel_id=1, source_target_pairs={{0,13},{1,12},{2,15},{3,14},{4,9},{5,8},{6,11},{7,10},{8,5},{9,4},... | collective-permute-start | bytes 2359304 | tf_op jit(solution)/shard_map/ppermute | solution.py:21
  681.9 8.3 %copy-start.9 = (f32[768]{0:T(1024)S(1)}, f32[768]{0:T(1024)}, u32[]{:S(2)}) copy-start(f32[768]{0:T(1024)} %param.13) | copy-start | bytes 9220
  690.2 21.4 %copy-start.7 = (bf16[768,768]{1,0:T(8,128)(2,1)S(1)}, bf16[768,768]{1,0:T(8,128)(2,1)}, u32[]{:S(2)}) copy-start(bf16[768,768]{1,0:T(8,128)(2,1)} %param.15) | copy-start | bytes 3538948
  711.6 38.6 %copy-start.1 = (bf16[768,768]{1,0:T(8,128)(2,1)S(1)}, bf16[768,768]{1,0:T(8,128)(2,1)}, u32[]{:S(2)}) copy-start(bf16[768,768]{1,0:T(8,128)(2,1)} %param.14) | copy-start | bytes 3538948
